TPU v7x, 128 devices: a whole 4x4x4 slice. The times are simulated.
128 devices in a mesh: band: 8 (over x, y_lo), row: 16 (over z, y_hi, core).
Axes of the slice: x: 4, y: 4 (y_hi: 2, y_lo: 2; y = y_hi * 2 + y_lo), z: 4, core: 2. Of those that a mesh axis runs over, the one named last changes fastest.
Arguments:
- phase: float32 [4096, 4096], P('row'), may hold values from -3.140625 to 3.140625
- aperture: int32 [4096, 4096], P('row'), may hold values 0 or 1
- defocus_index: int32 [16], P('band'), may hold values from 0 to 3
- intensity: float32 [16, 512, 512], P('band', 'row'), may hold values from 0.1 to 3
Outputs:
- gradient: float32 [4096, 4096], P('row', 'band')
All inputs are finite; a program needn't handle non-finite values. No bound on the sum of `aperture` on one device may be relied on, other than what follows from the above.
Results may differ from a plain program's by a relative error of at most 0.0032.
Values may be sent and summed in bfloat16 or wider, within the bound.
No kernel may reach another device: no remote copies, remote signals or barrier semaphores. Data moves between devices by JAX's collectives and lax.ppermute only.
A program may use at most 128 MiB of HBM per device.

v0:
```python
import math
import jax
import jax.numpy as jnp
from jax import lax
from jax.sharding import PartitionSpec as P

defocus_strength = math.pi


def focal_table(wave_index, waves, focal_width, pupil_width):
    scale_ratio = 1.0 / (1.0 + wave_index.astype(jnp.float32) / waves)
    column = 2 * lax.broadcasted_iota(jnp.int32, (focal_width, pupil_width), 1) - pupil_width + 1
    offset = 2 * lax.broadcasted_iota(jnp.int32, (focal_width, pupil_width), 0) - focal_width
    phase_angle = (column * offset).astype(jnp.float32) * (
        scale_ratio * (math.pi / (4.0 * pupil_width))
    )
    normalizer = 1.0 / math.sqrt(pupil_width)
    return jnp.stack(
        [jnp.cos(phase_angle) * normalizer, -jnp.sin(phase_angle) * normalizer]
    ).astype(jnp.bfloat16)


def pupil_field(phase, aperture, defocus_level, first_row, pupil_width):
    row_pos = (
        2 * (first_row + lax.broadcasted_iota(jnp.int32, phase.shape, 0)) - pupil_width + 1
    ).astype(jnp.float32)
    col_pos = (2 * lax.broadcasted_iota(jnp.int32, phase.shape, 1) - pupil_width + 1).astype(
        jnp.float32
    )
    radius = (row_pos * row_pos + col_pos * col_pos) / float(pupil_width * pupil_width)
    shifted = phase + defocus_level.astype(jnp.float32) * defocus_strength * radius
    amplitude = aperture.astype(jnp.float32)
    return (amplitude * jnp.cos(shifted), amplitude * jnp.sin(shifted))


def pupil_products(pupil_pair, table):
    blocks = lax.dot_general(
        pupil_pair, table, (((2,), (2,)), ((), ())), preferred_element_type=jnp.float32
    )
    real_part = blocks[0, :, 0] - blocks[1, :, 1]
    imag_part = blocks[0, :, 1] + blocks[1, :, 0]
    return jnp.stack([real_part, imag_part]).astype(jnp.bfloat16)


def focal_rows(products, table_cols):
    blocks = lax.dot_general(
        products, table_cols, (((1,), (2,)), ((), ())), preferred_element_type=jnp.float32
    )
    real_part = blocks[0, :, 0] - blocks[1, :, 1]
    imag_part = blocks[0, :, 1] + blocks[1, :, 0]
    return jnp.concatenate([real_part, imag_part], axis=1)


def back_rows(weighted, table_cols):
    unit_count = weighted.shape[0]
    table_width = table_cols.shape[1]
    halves = weighted.reshape(unit_count, 2, table_width)
    blocks = lax.dot_general(
        halves, table_cols, (((2,), (1,)), ((), ())), preferred_element_type=jnp.float32
    )
    real_part = blocks[:, 0, 0] + blocks[:, 1, 1]
    imag_part = blocks[:, 1, 0] - blocks[:, 0, 1]
    return jnp.stack([real_part, imag_part]).astype(jnp.bfloat16)


def phase_gradient(back, table, field_re, field_im):
    blocks = lax.dot_general(
        back, table, (((1,), (1,)), ((), ())), preferred_element_type=jnp.float32
    )
    spread_re = blocks[0, :, 0] + blocks[1, :, 1]
    spread_im = blocks[1, :, 0] - blocks[0, :, 1]
    return spread_im * field_re - spread_re * field_im


def local(phase, aperture, defocus_index, intensity):
    row_count = phase.shape[0]
    pupil_width = phase.shape[1]
    local_waves = intensity.shape[0]
    focal_width = intensity.shape[2]
    first_row = lax.axis_index("row") * row_count
    band_start = lax.axis_index("band") * local_waves
    total_waves = local_waves * lax.axis_size("band")
    running = jnp.zeros((row_count, pupil_width), jnp.float32)
    for member in range(local_waves):
        wave_index = band_start + member
        table = focal_table(wave_index, total_waves, focal_width, pupil_width)
        field_re, field_im = pupil_field(
            phase, aperture, defocus_index[member], first_row, pupil_width
        )
        pupil_pair = jnp.stack([field_re, field_im]).astype(jnp.bfloat16)
        products = pupil_products(pupil_pair, table)
        table_cols = lax.dynamic_slice_in_dim(table, first_row, row_count, 2)
        focal = lax.psum_scatter(
            focal_rows(products, table_cols), "row", scatter_dimension=0, tiled=True
        )
        focal_re = focal[:, :focal_width]
        focal_im = focal[:, focal_width:]
        misfit = focal_re * focal_re + focal_im * focal_im - intensity[member]
        weighted = jnp.concatenate([misfit * focal_re, misfit * focal_im], axis=1).astype(
            jnp.bfloat16
        )
        back = back_rows(lax.all_gather(weighted, "row", axis=0, tiled=True), table_cols)
        gradient = phase_gradient(back, table, field_re, field_im)
        running = running + gradient
    return lax.psum_scatter(running, "band", scatter_dimension=1, tiled=True)


def solution(mesh):
    return jax.shard_map(
        local,
        mesh=mesh,
        in_specs=(P("row", None), P("row", None), P("band"), P("band", "row", None)),
        out_specs=P("row", "band"),
        check_vma=False,
    )
```

profile of v0, /device:TPU:1, one launch (start us, length us, event | category | flops | bytes accessed | tf_op | source)
XLA Modules:
  0.0 509.1 jit_solution(2497417982271974181)
XLA Ops:
  6.7 1.3 fusion.75
  9.3 62.6 %multiply_convert_fusion.3 = (bf16[1,512,4096]{2,1,0:T(8,128)(2,1)}, bf16[1,512,4096]{2,1,0:T(8,128)(2,1)S(1)}, bf16[1,512,4096]{2,1,0:T(8,128)(2,1)S(1)}, bf16[1,512,4096]{2,1,0:T(8,128)(2,1)}) fusion(f32[]{:T(128)S(6)} %mul.229, s32[512]{0:T(512)S(1)} %multiply_add_fusion.1, s32[4096]{0:T(1024)S(1)} %multiply_add_fusion, f32[]{:T(128)S(6)} %mul.246), kind=kLoop, calls=%fused_computation.11 | loop fusion | flops 29360128 | bytes 16795656 | tf_op jit(solution)/shard_map/convert.26
  71.9 31.9 %convert_bitcast_fusion.3 = (bf16[1,256,4096]{2,1,0:T(8,128)(2,1)}, bf16[1,256,4096]{2,1,0:T(8,128)(2,1)}, bf16[1,256,4096]{2,1,0:T(8,128)(2,1)S(1)}, bf16[1,256,4096]{2,1,0:T(8,128)(2,1)S(1)}) fusion(f32[256,4096]{1,0:T(8,128)S(1)} %copy-done.8, f32[]{:T(128)} %bitcast, f32[4096]{0:T(1024)S(1)} %convert_multiply_fusion.2, ...), kind=kLoop, calls=%fused_computation.52 | loop fusion | flops 14680064 | bytes 16794632 | tf_op jit(solution)/shard_map/stack | solution.py:90
  103.8 4.5 fusion.8
  108.3 0.2 fusion.61
  108.5 1.7 fusion.46
  110.3 0.5 fusion.28
  110.7 0.2 pad_maximum_fusion.3
  110.9 1.9 copy.59
  112.9 9.3 %fusion.4 = f32[2,256,2,512]{3,1,2,0:T(8,128)S(1)} fusion(bf16[1,512,4096]{2,1,0:T(8,128)(2,1)} %get-tuple-element.30, bf16[1,512,4096]{2,1,0:T(8,128)(2,1)} %get-tuple-element.27, bf16[1,256,4096]{2,1,0:T(8,128)(2,1)} %get-tuple-element.6, bf16[1,256,4096]{2,1,0:T(8,128)(2,1)} %get-tuple-element.5), kind=kOutput, calls=%fused_computation.17 | convolution fusion | flops 4320133120 | bytes 14680064 | tf_op jit(solution)/shard_map/dot_general | solution.py:37
  122.2 0.2 fusion.57
  122.4 0.7 fusion.41
  123.1 0.5 fusion.30
  123.6 0.2 pad_maximum_fusion.2
  123.8 1.8 copy.57
  125.7 59.7 %reduce-scatter.12.cloned.1.call-done = f32[32,1024]{1,0:T(8,128)} async-done(((f32[512,1024]{1,0:T(8,128)}), f32[32,1024]{1,0:T(8,128)}) %reduce-scatter.12.cloned.1.call-update) | async-done | bytes 131088 | tf_op jit(solution)/shard_map/reduce_scatter | solution.py:93
  185.4 74.5 %reduce-scatter.10.cloned.1.call-done = f32[32,1024]{1,0:T(8,128)} async-done(((f32[512,1024]{1,0:T(8,128)}), f32[32,1024]{1,0:T(8,128)}) %reduce-scatter.10.cloned.1.call-update) | async-done | bytes 131088 | tf_op jit(solution)/shard_map/reduce_scatter | solution.py:93
  259.9 1.0 multiply_convert_fusion.7
  260.9 0.6 pad_maximum_fusion.5
  261.6 0.6 pad_maximum_fusion.4
  262.3 46.4 %all-gather.5.cloned.1.call-done = bf16[512,1024]{1,0:T(8,128)(2,1)} async-done(((bf16[32,1024]{1,0:T(8,128)(2,1)}), bf16[512,1024]{1,0:T(8,128)(2,1)}) %all-gather.5.cloned.1.call-update) | async-done | bytes 1048592 | tf_op jit(solution)/shard_map/all_gather | solution.py:102
  308.7 1.5 copy.38
  310.2 1.8 fusion.51
  312.1 42.6 %all-gather.3.cloned.1.call-done = bf16[512,1024]{1,0:T(8,128)(2,1)} async-done(((bf16[32,1024]{1,0:T(8,128)(2,1)}), bf16[512,1024]{1,0:T(8,128)(2,1)}) %all-gather.3.cloned.1.call-update) | async-done | bytes 1048592 | tf_op jit(solution)/shard_map/all_gather | solution.py:102
  354.7 1.5 copy.33
  356.2 1.9 fusion.54
  358.2 0.3 copy-done.5
  358.5 1.3 copy-done.7
  359.8 8.2 %fusion.2 = f32[2,256,2,4096]{3,1,2,0:T(8,128)} fusion(bf16[1,512,4096]{2,1,0:T(8,128)(2,1)S(1)} %copy-done.7, bf16[1,512,4096]{2,1,0:T(8,128)(2,1)S(1)} %copy-done.5, bf16[1,512,256]{2,1,0:T(8,128)(2,1)S(1)} %get-tuple-element.14, bf16[1,512,256]{2,1,0:T(8,128)(2,1)S(1)} %get-tuple-element.13), kind=kOutput, calls=%fused_computation.16 | convolution fusion | flops 4312793088 | bytes 25690112 | tf_op jit(solution)/shard_map/dot_general | solution.py:67
  368.0 8.2 %fusion.6 = f32[2,256,2,4096]{3,1,2,0:T(8,128)} fusion(bf16[1,512,4096]{2,1,0:T(8,128)(2,1)S(1)} %copy-done.3, bf16[1,512,4096]{2,1,0:T(8,128)(2,1)S(1)} %copy-done.1, bf16[1,512,256]{2,1,0:T(8,128)(2,1)S(1)} %get-tuple-element.18, bf16[1,512,256]{2,1,0:T(8,128)(2,1)S(1)} %get-tuple-element.17), kind=kOutput, calls=%fused_computation.18 | convolution fusion | flops 4312793088 | bytes 25690112 | tf_op jit(solution)/shard_map/dot_general | solution.py:67
  376.1 37.7 %fusion.15 = f32[256,4096]{1,0:T(8,128)} fusion(f32[2,256,2,4096]{3,1,2,0:T(8,128)} %fusion.6, f32[2,256,2,4096]{3,1,2,0:T(8,128)} %fusion.2, f32[256,4096]{1,0:T(8,128)S(1)} %copy-done.9, f32[]{:T(128)} %bitcast, f32[4096]{0:T(1024)S(1)} %convert_multiply_fusion.2, f32[256]{0:T(256)S(1)} %convert_multiply_fusion.3, s32[256,4096]{1,0:T(8,128)S(1)} %copy-done.11, ...), kind=kLoop, calls=%fused_computation.26 | loop fusion | flops 22020096 | bytes 46154760 | tf_op jit(solution)/shard_map/add | solution.py:104
  413.9 88.6 %reduce-scatter.8.cloned.1.call-done = f32[256,512]{1,0:T(8,128)} async-done(((f32[256,4096]{1,0:T(8,128)}), f32[256,512]{1,0:T(8,128)}) %reduce-scatter.8.cloned.1.call-update) | async-done | bytes 524304 | tf_op jit(solution)/shard_map/reduce_scatter | solution.py:105
  (40 shorter events, 0.6 us)
Async XLA Ops:
  6.5 178.9 %reduce-scatter.12.cloned.1.call-start = ((), (), s32[]{:S(2)}) async-start(), calls=%async_computation.7 | async-start | bytes 2228224 | tf_op jit(solution)/shard_map/reduce_scatter | solution.py:93
  9.3 62.6 %copy-start.8 = (f32[256,4096]{1,0:T(8,128)S(1)}, f32[256,4096]{1,0:T(8,128)}, u32[]{:S(2)}) copy-start(f32[256,4096]{1,0:T(8,128)} %param.4) | copy-start | bytes 12582916
  9.3 62.6 %copy-start.10 = (s32[256,4096]{1,0:T(8,128)S(1)}, s32[256,4096]{1,0:T(8,128)}, u32[]{:S(2)}) copy-start(s32[256,4096]{1,0:T(8,128)} %param.5) | copy-start | bytes 12582916
  71.9 31.9 %copy-start = (bf16[1,512,4096]{2,1,0:T(8,128)(2,1)}, bf16[1,512,4096]{2,1,0:T(8,128)(2,1)S(1)}, u32[]{:S(2)}) copy-start(bf16[1,512,4096]{2,1,0:T(8,128)(2,1)S(1)} %get-tuple-element.28) | copy-start | bytes 12582916
  71.9 31.9 %copy-start.2 = (bf16[1,512,4096]{2,1,0:T(8,128)(2,1)}, bf16[1,512,4096]{2,1,0:T(8,128)(2,1)S(1)}, u32[]{:S(2)}) copy-start(bf16[1,512,4096]{2,1,0:T(8,128)(2,1)S(1)} %get-tuple-element.29) | copy-start | bytes 12582916
  112.8 147.1 %reduce-scatter.10.cloned.1.call-start = ((), (), s32[]{:S(2)}) async-start(), calls=%async_computation.6 | async-start | bytes 2228224 | tf_op jit(solution)/shard_map/reduce_scatter | solution.py:93
  112.9 9.5 %copy-start.4 = (bf16[1,512,4096]{2,1,0:T(8,128)(2,1)S(1)}, bf16[1,512,4096]{2,1,0:T(8,128)(2,1)}, u32[]{:S(2)}) copy-start(bf16[1,512,4096]{2,1,0:T(8,128)(2,1)} %get-tuple-element.27) | copy-start | bytes 12582916
  112.9 9.5 %copy-start.6 = (bf16[1,512,4096]{2,1,0:T(8,128)(2,1)S(1)}, bf16[1,512,4096]{2,1,0:T(8,128)(2,1)}, u32[]{:S(2)}) copy-start(bf16[1,512,4096]{2,1,0:T(8,128)(2,1)} %get-tuple-element.30) | copy-start | bytes 12582916
  123.8 136.1 %copy-start.12 = (f32[2,32,512]{2,1,0:T(8,128)S(1)}, f32[2,32,512]{2,1,0:T(8,128)}, u32[]{:S(2)}) copy-start(f32[2,32,512]{2,1,0:T(8,128)} %param.7) | copy-start | bytes 393220
  125.6 183.0 %all-gather.5.cloned.1.call-start = ((), (), s32[]{:S(2)}) async-start(), calls=%async_computation.4 | async-start | bytes 1114112 | tf_op jit(solution)/shard_map/all_gather | solution.py:102
  261.5 93.1 %all-gather.3.cloned.1.call-start = ((), (), s32[]{:S(2)}) async-start(), calls=%async_computation.3 | async-start | bytes 1114112 | tf_op jit(solution)/shard_map/all_gather | solution.py:102
  262.2 240.3 %reduce-scatter.8.cloned.1.call-start = ((), (), s32[]{:S(2)}) async-start(), calls=%async_computation.5 | async-start | bytes 4718592 | tf_op jit(solution)/shard_map/reduce_scatter | solution.py:105
  356.2 2.4 copy-start.5
  356.2 3.6 copy-start.7
  359.8 8.2 %copy-start.1 = (bf16[1,512,4096]{2,1,0:T(8,128)(2,1)S(1)}, bf16[1,512,4096]{2,1,0:T(8,128)(2,1)}, u32[]{:S(2)}) copy-start(bf16[1,512,4096]{2,1,0:T(8,128)(2,1)} %copy-done) | copy-start | bytes 12582916
  359.8 8.2 %copy-start.3 = (bf16[1,512,4096]{2,1,0:T(8,128)(2,1)S(1)}, bf16[1,512,4096]{2,1,0:T(8,128)(2,1)}, u32[]{:S(2)}) copy-start(bf16[1,512,4096]{2,1,0:T(8,128)(2,1)} %copy-done.2) | copy-start | bytes 12582916
  368.0 8.2 %copy-start.9 = (f32[256,4096]{1,0:T(8,128)S(1)}, f32[256,4096]{1,0:T(8,128)}, u32[]{:S(2)}) copy-start(f32[256,4096]{1,0:T(8,128)} %param.4) | copy-start | bytes 12582916
  368.0 8.2 %copy-start.11 = (s32[256,4096]{1,0:T(8,128)S(1)}, s32[256,4096]{1,0:T(8,128)}, u32[]{:S(2)}) copy-start(s32[256,4096]{1,0:T(8,128)} %param.5) | copy-start | bytes 12582916
Sparse Core Ops, SparseCore 0:
  112.9 72.4 reduce-scatter.11
  189.8 70.0 reduce-scatter.9
  262.4 46.2 all-gather.4
  311.0 43.6 all-gather.2
  414.0 88.4 reduce-scatter.7
where the time goes:
time: 509 us
  waiting for transfers between devices  312 us (61%)
  other arithmetic  136 us (27%)
  matrix products  36.3 us (7%)
  between operations  14.7 us (3%)
  local copies, waits for them, and re-layouts  9.65 us (2%)
    reduce_scatter x2, waiting for transfers between devices, local(): lax.psum_scatter(focal_rows(products, table_cols), 'row', scatter_dimensi...  134 us
    all_gather x2, waiting for transfers between devices, local(): lax.all_gather(weighted, 'row', axis=0, tiled=True)  89 us
    reduce_scatter x1, waiting for transfers between devices, local(): return lax.psum_scatter(running, 'band', scatter_dimension=1, tiled=True)  88.6 us
    another operation x2, other arithmetic  63.5 us
    add x1, other arithmetic, local(): running = running + gradient  37.7 us
    another operation x1, other arithmetic, local(): pupil_pair = jnp.stack([field_re, field_im]).astype(jnp.bfloat16)  31.9 us
    dot_general x2, matrix products, phase_gradient(): lax.dot_general(back, table, (((1,), (1,)), ((), ())), preferred_element_...  16.3 us
    dot_general x2, matrix products, pupil_products(): lax.dot_general(pupil_pair, table, (((2,), (2,)), ((), ())), preferred_el...  13.8 us
  transfers between devices with their start and end apart: 5, of which 5 were waited for; matrix products, arithmetic and copies ran while one was open for 3% of the time, Pallas kernels for 0%

commit v1 on v0

--- a/solution.py
+++ b/solution.py
@@ -1,10 +1,23 @@
+import functools
 import math
 import jax
 import jax.numpy as jnp
 from jax import lax
 from jax.sharding import PartitionSpec as P
+from jax.lax import all_to_all, axis_size
 
 defocus_strength = math.pi
+
+
+def make_waves_for(patch, device_axis):
+    now = jnp.concatenate(
+        all_to_all(jnp.stack([patch for _ in range(axis_size(device_axis))]), device_axis, 0, 0),
+        axis=0,
+    )
+    return now
+
+
+test_samples = functools.partial(make_waves_for, device_axis="row")
 
 
 def focal_table(wave_index, waves, focal_width, pupil_width):
@@ -99,7 +112,7 @@
         weighted = jnp.concatenate([misfit * focal_re, misfit * focal_im], axis=1).astype(
             jnp.bfloat16
         )
-        back = back_rows(lax.all_gather(weighted, "row", axis=0, tiled=True), table_cols)
+        back = back_rows(test_samples(weighted), table_cols)
         gradient = phase_gradient(back, table, field_re, field_im)
         running = running + gradient
     return lax.psum_scatter(running, "band", scatter_dimension=1, tiled=True)

time: 509 us -> 462 us (0.908)
  waiting for transfers between devices: 312 us -> 253 us
  starting transfers between devices: 0.17 us -> 11.6 us
    all_gather x2 -> x0, waiting for transfers between devices: 89 us -> none  [local(): lax.all_gather(weighted, 'row', axis=0, tiled=True)]
    all_to_all x0 -> x2, waiting for transfers between devices: none -> 31.8 us  [make_waves_for(): all_to_all(jnp.stack([patch for _ in range(axis_size(device_axis))]), dev...]
    all_to_all x0 -> x2, starting transfers between devices: none -> 11.5 us  [make_waves_for(): all_to_all(jnp.stack([patch for _ in range(axis_size(device_axis))]), dev...]
where the time goes in v1:
time: 462 us
  waiting for transfers between devices  253 us (55%)
  other arithmetic  135 us (29%)
  matrix products  36.3 us (8%)
  between operations  14.8 us (3%)
  starting transfers between devices  11.6 us (3%)
  local copies, waits for them, and re-layouts  10.7 us (2%)
    reduce_scatter x2, waiting for transfers between devices, local(): lax.psum_scatter(focal_rows(products, table_cols), 'row', scatter_dimensi...  134 us
    reduce_scatter x1, waiting for transfers between devices, local(): return lax.psum_scatter(running, 'band', scatter_dimension=1, tiled=True)  87.4 us
    another operation x2, other arithmetic  63.5 us
    add x1, other arithmetic, local(): running = running + gradient  37.7 us
    another operation x1, other arithmetic, local(): pupil_pair = jnp.stack([field_re, field_im]).astype(jnp.bfloat16)  31.9 us
    all_to_all x2, waiting for transfers between devices, make_waves_for(): all_to_all(jnp.stack([patch for _ in range(axis_size(device_axis))]), dev...  31.8 us
    dot_general x2, matrix products, phase_gradient(): lax.dot_general(back, table, (((1,), (1,)), ((), ())), preferred_element_...  16.3 us
    dot_general x2, matrix products, pupil_products(): lax.dot_general(pupil_pair, table, (((2,), (2,)), ((), ())), preferred_el...  13.8 us
  transfers between devices with their start and end apart: 5, of which 5 were waited for; matrix products, arithmetic and copies ran while one was open for 3% of the time, Pallas kernels for 0%

profile of v1, /device:TPU:1, one launch (start us, length us, event | category | flops | bytes accessed | tf_op | source)
XLA Modules:
  0.0 461.8 jit_solution(15885560212896807333)
XLA Ops:
  6.7 1.4 fusion.77
  9.4 62.6 %multiply_convert_fusion.3 = (bf16[1,512,4096]{2,1,0:T(8,128)(2,1)}, bf16[1,512,4096]{2,1,0:T(8,128)(2,1)S(1)}, bf16[1,512,4096]{2,1,0:T(8,128)(2,1)S(1)}, bf16[1,512,4096]{2,1,0:T(8,128)(2,1)}) fusion(f32[]{:T(128)S(6)} %mul.229, s32[512]{0:T(512)S(1)} %multiply_add_fusion.1, s32[4096]{0:T(1024)S(1)} %multiply_add_fusion, f32[]{:T(128)S(6)} %mul.246), kind=kLoop, calls=%fused_computation.11 | loop fusion | flops 29360128 | bytes 16795656 | tf_op jit(solution)/shard_map/convert.26
  72.0 31.9 %convert_bitcast_fusion.3 = (bf16[1,256,4096]{2,1,0:T(8,128)(2,1)}, bf16[1,256,4096]{2,1,0:T(8,128)(2,1)}, bf16[1,256,4096]{2,1,0:T(8,128)(2,1)S(1)}, bf16[1,256,4096]{2,1,0:T(8,128)(2,1)S(1)}) fusion(f32[256,4096]{1,0:T(8,128)S(1)} %copy-done.8, f32[]{:T(128)} %bitcast, f32[4096]{0:T(1024)S(1)} %convert_multiply_fusion.2, ...), kind=kLoop, calls=%fused_computation.52 | loop fusion | flops 14680064 | bytes 16794632 | tf_op jit(solution)/shard_map/stack | solution.py:103
  103.9 4.5 fusion.8
  108.6 1.7 fusion.50
  110.3 0.5 fusion.28
  110.8 0.2 pad_maximum_fusion.3
  111.0 1.9 copy.55
  113.0 9.3 %fusion.4 = f32[2,256,2,512]{3,1,2,0:T(8,128)S(1)} fusion(bf16[1,512,4096]{2,1,0:T(8,128)(2,1)} %get-tuple-element.30, bf16[1,512,4096]{2,1,0:T(8,128)(2,1)} %get-tuple-element.27, bf16[1,256,4096]{2,1,0:T(8,128)(2,1)} %get-tuple-element.6, bf16[1,256,4096]{2,1,0:T(8,128)(2,1)} %get-tuple-element.5), kind=kOutput, calls=%fused_computation.17 | convolution fusion | flops 4320133120 | bytes 14680064 | tf_op jit(solution)/shard_map/dot_general | solution.py:50
  122.5 0.7 fusion.45
  123.2 0.5 fusion.30
  123.7 0.2 pad_maximum_fusion.2
  123.9 1.8 copy.53
  125.7 59.8 %reduce-scatter.12.cloned.1.call-done = f32[32,1024]{1,0:T(8,128)} async-done(((f32[512,1024]{1,0:T(8,128)}), f32[32,1024]{1,0:T(8,128)}) %reduce-scatter.12.cloned.1.call-update) | async-done | bytes 131088 | tf_op jit(solution)/shard_map/reduce_scatter | solution.py:106
  185.5 74.5 %reduce-scatter.10.cloned.1.call-done = f32[32,1024]{1,0:T(8,128)} async-done(((f32[512,1024]{1,0:T(8,128)}), f32[32,1024]{1,0:T(8,128)}) %reduce-scatter.10.cloned.1.call-update) | async-done | bytes 131088 | tf_op jit(solution)/shard_map/reduce_scatter | solution.py:106
  260.0 1.0 multiply_convert_fusion.7
  261.0 1.2 stack.45
  262.2 7.1 %all-to-all-start = ((bf16[16,32,1024]{2,1,0:T(8,128)(2,1)}), bf16[16,32,1024]{2,1,0:T(8,128)(2,1)S(1)}, u32[]{:S(2)}, u32[]{:S(2)}) async-start(bf16[16,32,1024]{2,1,0:T(8,128)(2,1)} %stack.45), calls=%async_computation | async-start | bytes 2097152 | tf_op jit(solution)/shard_map/all_to_all | solution.py:14
  269.3 17.2 %all-to-all-done = bf16[16,32,1024]{2,1,0:T(8,128)(2,1)S(1)} async-done(((bf16[16,32,1024]{2,1,0:T(8,128)(2,1)}), bf16[16,32,1024]{2,1,0:T(8,128)(2,1)S(1)}, u32[]{:S(2)}, u32[]{:S(2)}) %all-to-all-start) | async-done | bytes 1048608 | tf_op jit(solution)/shard_map/all_to_all | solution.py:14
  286.5 1.2 stack.52
  287.7 4.4 all-to-all-start.1
  292.1 0.8 reshape_reshape.6
  292.9 1.7 fusion.33
  294.8 14.6 %all-to-all-done.1 = bf16[16,32,1024]{2,1,0:T(8,128)(2,1)S(1)} async-done(((bf16[16,32,1024]{2,1,0:T(8,128)(2,1)}), bf16[16,32,1024]{2,1,0:T(8,128)(2,1)S(1)}, u32[]{:S(2)}, u32[]{:S(2)}) %all-to-all-start.1) | async-done | bytes 1048608 | tf_op jit(solution)/shard_map/all_to_all | solution.py:14
  309.4 0.8 reshape_reshape.7
  310.2 1.9 fusion.31
  312.2 0.3 copy-done.5
  312.5 1.3 copy-done.7
  313.8 8.1 %fusion.6 = f32[2,256,2,4096]{3,1,2,0:T(8,128)} fusion(bf16[1,512,4096]{2,1,0:T(8,128)(2,1)S(1)} %copy-done.7, bf16[1,512,4096]{2,1,0:T(8,128)(2,1)S(1)} %copy-done.5, bf16[1,512,256]{2,1,0:T(8,128)(2,1)S(1)} %get-tuple-element.18, bf16[1,512,256]{2,1,0:T(8,128)(2,1)S(1)} %get-tuple-element.17), kind=kOutput, calls=%fused_computation.18 | convolution fusion | flops 4312793088 | bytes 25690112 | tf_op jit(solution)/shard_map/dot_general | solution.py:80
  322.0 8.2 %fusion.2 = f32[2,256,2,4096]{3,1,2,0:T(8,128)} fusion(bf16[1,512,4096]{2,1,0:T(8,128)(2,1)S(1)} %copy-done.3, bf16[1,512,4096]{2,1,0:T(8,128)(2,1)S(1)} %copy-done.1, bf16[1,512,256]{2,1,0:T(8,128)(2,1)S(1)} %get-tuple-element.14, bf16[1,512,256]{2,1,0:T(8,128)(2,1)S(1)} %get-tuple-element.13), kind=kOutput, calls=%fused_computation.16 | convolution fusion | flops 4312793088 | bytes 25690112 | tf_op jit(solution)/shard_map/dot_general | solution.py:80
  330.2 37.7 %fusion.15 = f32[256,4096]{1,0:T(8,128)} fusion(f32[2,256,2,4096]{3,1,2,0:T(8,128)} %fusion.6, f32[2,256,2,4096]{3,1,2,0:T(8,128)} %fusion.2, f32[256,4096]{1,0:T(8,128)S(1)} %copy-done.9, f32[]{:T(128)} %bitcast, f32[4096]{0:T(1024)S(1)} %convert_multiply_fusion.2, f32[256]{0:T(256)S(1)} %convert_multiply_fusion.3, s32[256,4096]{1,0:T(8,128)S(1)} %copy-done.11, ...), kind=kLoop, calls=%fused_computation.26 | loop fusion | flops 22020096 | bytes 46154760 | tf_op jit(solution)/shard_map/add | solution.py:117
  367.9 87.4 %reduce-scatter.8.cloned.1.call-done = f32[256,512]{1,0:T(8,128)} async-done(((f32[256,4096]{1,0:T(8,128)}), f32[256,512]{1,0:T(8,128)}) %reduce-scatter.8.cloned.1.call-update) | async-done | bytes 524304 | tf_op jit(solution)/shard_map/reduce_scatter | solution.py:118
  (40 shorter events, 0.8 us)
Async XLA Ops:
  6.5 179.0 %reduce-scatter.12.cloned.1.call-start = ((), (), s32[]{:S(2)}) async-start(), calls=%async_computation.7 | async-start | bytes 2228224 | tf_op jit(solution)/shard_map/reduce_scatter | solution.py:106
  9.4 62.6 %copy-start.8 = (f32[256,4096]{1,0:T(8,128)S(1)}, f32[256,4096]{1,0:T(8,128)}, u32[]{:S(2)}) copy-start(f32[256,4096]{1,0:T(8,128)} %param.4) | copy-start | bytes 12582916
  9.4 62.6 %copy-start.10 = (s32[256,4096]{1,0:T(8,128)S(1)}, s32[256,4096]{1,0:T(8,128)}, u32[]{:S(2)}) copy-start(s32[256,4096]{1,0:T(8,128)} %param.5) | copy-start | bytes 12582916
  72.0 31.9 %copy-start.4 = (bf16[1,512,4096]{2,1,0:T(8,128)(2,1)}, bf16[1,512,4096]{2,1,0:T(8,128)(2,1)S(1)}, u32[]{:S(2)}) copy-start(bf16[1,512,4096]{2,1,0:T(8,128)(2,1)S(1)} %get-tuple-element.28) | copy-start | bytes 12582916
  72.0 31.9 %copy-start.6 = (bf16[1,512,4096]{2,1,0:T(8,128)(2,1)}, bf16[1,512,4096]{2,1,0:T(8,128)(2,1)S(1)}, u32[]{:S(2)}) copy-start(bf16[1,512,4096]{2,1,0:T(8,128)(2,1)S(1)} %get-tuple-element.29) | copy-start | bytes 12582916
  112.9 147.1 %reduce-scatter.10.cloned.1.call-start = ((), (), s32[]{:S(2)}) async-start(), calls=%async_computation.6 | async-start | bytes 2228224 | tf_op jit(solution)/shard_map/reduce_scatter | solution.py:106
  113.0 9.5 %copy-start = (bf16[1,512,4096]{2,1,0:T(8,128)(2,1)S(1)}, bf16[1,512,4096]{2,1,0:T(8,128)(2,1)}, u32[]{:S(2)}) copy-start(bf16[1,512,4096]{2,1,0:T(8,128)(2,1)} %get-tuple-element.27) | copy-start | bytes 12582916
  113.0 9.5 %copy-start.2 = (bf16[1,512,4096]{2,1,0:T(8,128)(2,1)S(1)}, bf16[1,512,4096]{2,1,0:T(8,128)(2,1)}, u32[]{:S(2)}) copy-start(bf16[1,512,4096]{2,1,0:T(8,128)(2,1)} %get-tuple-element.30) | copy-start | bytes 12582916
  123.9 136.1 %copy-start.12 = (f32[2,32,512]{2,1,0:T(8,128)S(1)}, f32[2,32,512]{2,1,0:T(8,128)}, u32[]{:S(2)}) copy-start(f32[2,32,512]{2,1,0:T(8,128)} %param.7) | copy-start | bytes 393220
  262.2 24.4 %all-to-all-start = ((bf16[16,32,1024]{2,1,0:T(8,128)(2,1)}), bf16[16,32,1024]{2,1,0:T(8,128)(2,1)S(1)}, u32[]{:S(2)}, u32[]{:S(2)}) async-start(bf16[16,32,1024]{2,1,0:T(8,128)(2,1)} %stack.45), calls=%async_computation | async-start | bytes 2097152 | tf_op jit(solution)/shard_map/all_to_all | solution.py:14
  287.7 21.6 %all-to-all-start.1 = ((bf16[16,32,1024]{2,1,0:T(8,128)(2,1)}), bf16[16,32,1024]{2,1,0:T(8,128)(2,1)S(1)}, u32[]{:S(2)}, u32[]{:S(2)}) async-start(bf16[16,32,1024]{2,1,0:T(8,128)(2,1)} %stack.52), calls=%async_computation.1 | async-start | bytes 2097152 | tf_op jit(solution)/shard_map/all_to_all | solution.py:14
  292.1 163.2 %reduce-scatter.8.cloned.1.call-start = ((), (), s32[]{:S(2)}) async-start(), calls=%async_computation.5 | async-start | bytes 4718592 | tf_op jit(solution)/shard_map/reduce_scatter | solution.py:118
  310.2 2.4 copy-start.5
  310.2 3.6 copy-start.7
  313.8 8.1 %copy-start.1 = (bf16[1,512,4096]{2,1,0:T(8,128)(2,1)S(1)}, bf16[1,512,4096]{2,1,0:T(8,128)(2,1)}, u32[]{:S(2)}) copy-start(bf16[1,512,4096]{2,1,0:T(8,128)(2,1)} %get-tuple-element.27) | copy-start | bytes 12582916
  313.8 8.1 %copy-start.3 = (bf16[1,512,4096]{2,1,0:T(8,128)(2,1)S(1)}, bf16[1,512,4096]{2,1,0:T(8,128)(2,1)}, u32[]{:S(2)}) copy-start(bf16[1,512,4096]{2,1,0:T(8,128)(2,1)} %get-tuple-element.30) | copy-start | bytes 12582916
  322.0 8.2 %copy-start.9 = (f32[256,4096]{1,0:T(8,128)S(1)}, f32[256,4096]{1,0:T(8,128)}, u32[]{:S(2)}) copy-start(f32[256,4096]{1,0:T(8,128)} %param.4) | copy-start | bytes 12582916
  322.0 8.2 %copy-start.11 = (s32[256,4096]{1,0:T(8,128)S(1)}, s32[256,4096]{1,0:T(8,128)}, u32[]{:S(2)}) copy-start(s32[256,4096]{1,0:T(8,128)} %param.5) | copy-start | bytes 12582916
Sparse Core Ops, SparseCore 0:
  113.0 72.4 reduce-scatter.11
  189.9 70.0 reduce-scatter.9
  368.0 87.1 reduce-scatter.7
